TPU v7x, 32 devices: a whole 2x2x4 slice. The times are simulated.
32 devices in a mesh: tile: 8 (over z, x), chan: 4 (over y, core).
Axes of the slice: x: 2, y: 2, z: 4, core: 2. Of those that a mesh axis runs over, the one named last changes fastest.
Arguments:
- features: bfloat16 [64, 64, 4096], P('tile', 'chan'), may hold values from -6 to 6
- conv_weight: bfloat16 [64, 576], P('chan'), may hold values from -0.25 to 0.25
- conv_bias: float32 [64], P('chan'), may hold values from -3 to 3
- down_weight: bfloat16 [64, 256], P(None, 'chan'), may hold values from -0.375 to 0.375
- cotangent: bfloat16 [16, 64, 4096], P('tile', 'chan'), may hold values from -0.0234375 to 0.0234375
- edge_links: int32 [64, 4], P('tile'), may hold values from 0 to 63, as said below
- edge_turns: int32 [64, 4], P('tile'), may hold values from 0 to 3
- corner_links: int32 [64, 4], P('tile'), may hold values from -1 to 63, as said below
- corner_turns: int32 [64, 4], P('tile'), may hold values from 0 to 3
- child_slot: int32 [64], P('tile'), may hold values from 0 to 63, as said below
Outputs:
- coarse: bfloat16 [16, 64, 4096], P('tile', 'chan')
- grad_conv: float32 [64, 576], P('chan')
- grad_bias: float32 [64], P('chan')
- grad_down: float32 [64, 256], P(None, 'chan')
Inputs may be any that keep to these rules, and one draw needn't show every extreme that they name: `edge_links`: edge k: 0 north, 1 west, 2 south, 3 east. `corner_links`: corner k: 0 north-west, 1 south-west, 2 south-east, 3 north-east; -1 where no tile touches that corner. `child_slot`: a permutation of 0 to 63; coarse tile k lies on index k // 2 of tile; of the 8 fine tiles of one index of tile, at most 1 have their coarse tiles on any one index of tile, and that many do for some pair.
All inputs are finite; a program needn't handle non-finite values.
Results may differ from a plain program's by a relative error of at most 0.0055.
Values may be sent and summed in bfloat16 or wider, within the bound.
A program may use at most 64 MiB of HBM per device.

v0:
```python
import functools

import jax
import jax.numpy as jnp
import numpy as np
from jax import lax
from jax.experimental import pallas as pl
from jax.experimental.pallas import tpu as pltpu
from jax.sharding import PartitionSpec as P

C = 64
S = 64
H = S // 2
QUARTER = H * H
TAPS = 9
MESH = pl.DeviceIdType.MESH
F32 = jnp.float32
BF16 = jnp.bfloat16
VMEM_LIMIT = 50 * 1024 * 1024
PACK = 1024
BIAS_COL = TAPS * C
DOWN_COL = BIAS_COL + C
SLOT_LANE = 16


def rim_selector():
    pick = np.zeros((S * S, 4 * S), np.float32)
    for n in range(S):
        pick[S - 1 - n, n] = 1
        pick[n * S, S + n] = 1
        pick[(S - 1) * S + n, 2 * S + n] = 1
        pick[(S - 1 - n) * S + S - 1, 3 * S + n] = 1
    return pick


def phase_selector():
    lane = np.arange(8 * S)
    row, col = lane // S, lane % S
    target = ((row % 2) * 2 + col % 2) * 128 + (row // 2) * H + col // 2
    pick = np.zeros((8 * S, 8 * S), np.float32)
    pick[lane, target] = 1
    return pick


def half_selector():
    lane = np.arange(4 * S)
    row, col = lane // S, lane % S
    pick = np.zeros((4 * S, 4 * S), np.float32)
    pick[lane, (col // H) * 128 + row * H + col % H] = 1
    return pick


def side_selector():
    pick = np.zeros((2 * S, 4 * QUARTER), np.float32)
    for a in range(2):
        for u in range(H):
            pick[S - 1 - (2 * u + a), a * QUARTER + u * H] = 1
            pick[S + 2 * u + a, (2 + a) * QUARTER + u * H + H - 1] = 1
    return pick


def cap_selector():
    pick = np.zeros((4 * S, 8 * 128), np.float32)
    for wx in range(4):
        for v in range(H):
            x = 2 * v + wx - 1
            top = 128 + 0 if x < 0 else 128 + 3 if x >= S else x
            low = 128 + 1 if x < 0 else 128 + 2 if x >= S else S + S - 1 - x
            pick[top, wx * 128 + v] = 1
            pick[low, (4 + wx) * 128 + 96 + v] = 1
    return pick


def tap_selector():
    pick = np.zeros((C * TAPS, C * TAPS), np.float32)
    for i in range(C):
        for tap in range(TAPS):
            pick[i * TAPS + tap, tap * C + i] = 1
    return pick


def down_selector(n_chan):
    local = C // n_chan
    pick = np.zeros((n_chan, local * 4, C * 4), np.float32)
    for i in range(C):
        for ab in range(4):
            pick[i // local, (i % local) * 4 + ab, ab * C + i] = 1
    return pick


def dot(a, b):
    return jnp.dot(a, b, preferred_element_type=F32)


def dot_nt(a, b):
    return lax.dot_general(a, b, (((1,), (1,)), ((), ())), preferred_element_type=F32)


def split_dot_nt(a, selector):
    high = a.astype(BF16)
    rest = a - high.astype(F32)
    middle = rest.astype(BF16)
    low = (rest - middle.astype(F32)).astype(BF16)
    return dot_nt(high, selector) + dot_nt(middle, selector) + dot_nt(low, selector)


def greet(n_tile, n_chan, me_t, me_c):
    barrier = pltpu.get_barrier_semaphore()
    for k in range(1, n_tile):
        peer = lax.rem(me_t + k, n_tile)
        pl.semaphore_signal(barrier, inc=1, device_id=(peer, me_c), device_id_type=MESH)
    for k in range(1, n_chan):
        peer = lax.rem(me_c + k, n_chan)
        pl.semaphore_signal(barrier, inc=1, device_id=(me_t, peer), device_id_type=MESH)


def remote(src, dst, send_sem, recv_sem, device):
    copy = pltpu.make_async_remote_copy(
        src_ref=src,
        dst_ref=dst,
        send_sem=send_sem,
        recv_sem=recv_sem,
        device_id=device,
        device_id_type=MESH,
    )
    copy.start()
    return copy


def find_owners(table, groups, tiles, wanted):
    def step(s, found):
        for t in range(tiles):
            value = table[s, t, SLOT_LANE]
            found = tuple(jnp.where(value == w, s, f) for w, f in zip(wanted, found))
        return found

    return lax.fori_loop(0, groups, step, (jnp.int32(0),) * len(wanted))


def widen_weights(taps, wide):
    none = jnp.zeros((C, C), F32)
    for a in range(2):
        for b in range(2):
            pieces = []
            for wy in range(4):
                for wx in range(4):
                    dy, dx = wy - a, wx - b
                    if 0 <= dy < 3 and 0 <= dx < 3:
                        tap = 3 * dy + dx
                        pieces.append(taps[:, tap * C : tap * C + C])
                    else:
                        pieces.append(none)
            row = (a * 2 + b) * C
            wide[row : row + C, :] = jnp.concatenate(pieces, axis=1).astype(BF16)


def fill_window(phase, sides, caps, window, t):
    lane = lax.broadcasted_iota(jnp.int32, (C, QUARTER), 1)
    first_col = lax.rem(lane, H) == 0
    last_col = lax.rem(lane, H) == H - 1
    lane_cap = lax.broadcasted_iota(jnp.int32, (C, 128), 1)
    for a in range(2):
        even, odd = phase[a * 2], phase[a * 2 + 1]
        west = jnp.where(
            first_col, sides[:, a * QUARTER : (a + 1) * QUARTER], pltpu.roll(odd, 1, 1)
        )
        east = jnp.where(
            last_col,
            sides[:, (2 + a) * QUARTER : (3 + a) * QUARTER],
            pltpu.roll(even, QUARTER - 1, 1),
        )
        for wx, middle in enumerate((west, even, odd, east)):
            row = ((1 + a) * 4 + wx) * C
            window[t, row : row + C, :] = middle.astype(BF16)
            if a == 1:
                moved = pltpu.roll(middle, H, 1)
                cap = caps[:, wx * 128 : wx * 128 + 128]
                head = jnp.where(lane_cap < H, cap, moved[:, :128])
                moved = jnp.concatenate([head, moved[:, 128:]], axis=1)
                row = wx * C
            else:
                moved = pltpu.roll(middle, QUARTER - H, 1)
                cap = caps[:, (4 + wx) * 128 : (5 + wx) * 128]
                tail = jnp.where(lane_cap >= 128 - H, cap, moved[:, QUARTER - 128 :])
                moved = jnp.concatenate([moved[:, : QUARTER - 128], tail], axis=1)
                row = (12 + wx) * C
            window[t, row : row + C, :] = moved.astype(BF16)


def level_kernel(
    n_tile,
    n_chan,
    tiles,
    feat_hbm,
    cot_hbm,
    cw_hbm,
    dw_hbm,
    table_hbm,
    rim_sel_hbm,
    half_sel_hbm,
    phase_sel_hbm,
    side_sel_hbm,
    cap_sel_hbm,
    tap_sel_hbm,
    down_sel_hbm,
    cb_smem,
    placed_out,
    grads_out,
    feat,
    cot,
    rim_sel,
    half_sel,
    phase_sel,
    side_sel,
    cap_sel,
    tap_sel,
    down_sel,
    feat_all,
    cw_all,
    dw_all,
    cb_all,
    table_all,
    table,
    rims,
    halos,
    halo_all,
    slots,
    cot_send,
    cot_recv,
    cot_group,
    cot_all,
    wide,
    phases,
    window,
    pre_act,
    hidden,
    quarter,
    quarter_group,
    quarter_send,
    quarter_recv,
    pack,
    pack_recv,
    pieces,
    pieces_recv,
    local_sem,
    chan_send,
    chan_recv,
    tile_send,
    tile_recv,
    rim_send,
    rim_recv,
):
    me_t = lax.axis_index("tile")
    me_c = lax.axis_index("chan")
    per = tiles // n_chan
    local = feat.shape[1]
    n_outer = n_tile // 2
    outer, inner = me_t // 2, lax.rem(me_t, 2)

    greet(n_tile, n_chan, me_t, me_c)

    def fetch(src, dst, k):
        copy = pltpu.make_async_copy(src, dst, local_sem.at[k])
        copy.start()
        return copy

    get_feat = fetch(feat_hbm, feat, 0)
    get_rim_sel = fetch(rim_sel_hbm, rim_sel, 1)
    get_cot = fetch(cot_hbm, cot, 2)
    get_half_sel = fetch(half_sel_hbm, half_sel, 3)
    get_table = fetch(table_hbm, table_all.at[me_t], 4)
    get_own = [
        fetch(cw_hbm, cw_all.at[me_c], 5),
        fetch(dw_hbm, dw_all.at[me_c], 6),
        fetch(feat_hbm.at[pl.ds(me_c * per, per)], feat_all.at[me_c], 7),
        fetch(phase_sel_hbm, phase_sel, 8),
        fetch(side_sel_hbm, side_sel, 9),
        fetch(cap_sel_hbm, cap_sel, 10),
        fetch(tap_sel_hbm, tap_sel, 11),
        fetch(down_sel_hbm, down_sel, 12),
    ]
    row = lax.broadcasted_iota(jnp.int32, (local, 128), 0)
    bias = jnp.zeros((local, 128), F32)
    for n in range(local):
        bias = jnp.where(row == n, cb_smem[n], bias)
    cb_all[pl.ds(me_c, 1)] = bias[None]

    get_feat.wait()
    get_rim_sel.wait()
    pixels = feat[...].reshape(tiles * local, S * S)
    my_rims = dot(pixels, rim_sel[...]).astype(BF16)
    rims[pl.ds(me_t, 1)] = my_rims.reshape(1, tiles, local, 4 * S)
    get_table.wait()

    pl.semaphore_wait(pltpu.get_barrier_semaphore(), n_tile - 1 + n_chan - 1)

    def to_tiles(kind, src, dst):
        copies = []
        for k in range(1, n_tile):
            d = lax.rem(me_t + k, n_tile)
            copies.append(
                remote(
                    src(d), dst, tile_send.at[kind, k], tile_recv.at[kind, k], (d, me_c)
                )
            )
        return copies

    def to_chans(kind, src, dst):
        copies = []
        for k in range(1, n_chan):
            c = lax.rem(me_c + k, n_chan)
            copies.append(
                remote(
                    src(c), dst, chan_send.at[kind, k], chan_recv.at[kind, k], (me_t, c)
                )
            )
        return copies

    def finish(copies):
        for copy in copies:
            copy.wait()

    def chan_rows(c):
        return pl.ds(pl.multiple_of(c * local, local), local)

    table_copies = to_tiles(0, lambda d: table_all.at[me_t], table_all.at[me_t])
    across = outer * 2 + 1 - inner
    forwards = [
        remote(
            rims.at[me_t], rims.at[me_t], rim_send.at[1, 0], rim_recv.at[1, 0], (across, me_c)
        )
    ]
    straight = []
    for k in range(1, n_outer):
        d = lax.rem(outer + k, n_outer) * 2 + inner
        straight.append(
            remote(rims.at[me_t], rims.at[me_t], rim_send.at[0, k], rim_recv.at[0, k], (d, me_c))
        )
    small_copies = (
        to_chans(1, lambda c: cw_hbm, cw_all.at[me_c])
        + to_chans(2, lambda c: dw_hbm, dw_all.at[me_c])
        + to_chans(3, lambda c: cb_all.at[me_c], cb_all.at[me_c])
    )
    feat_copies = to_chans(0, lambda c: feat_hbm.at[pl.ds(c * per, per)], feat_all.at[me_c])

    get_cot.wait()
    get_half_sel.wait()
    coarse_tiles = cot.shape[0]
    cots = cot[...].reshape(coarse_tiles * local, S * S)
    for j in range(16):
        moved = dot(cots[:, 256 * j : 256 * j + 256], half_sel[...]).astype(BF16)
        lanes = slice((j % 8) * 128, (j % 8) * 128 + 128)
        for n in range(coarse_tiles):
            rows = moved[n * local : (n + 1) * local]
            slots[n * 4 + (j // 8) * 2, :, lanes] = rows[:, :128]
            slots[n * 4 + (j // 8) * 2 + 1, :, lanes] = rows[:, 128:]

    finish(table_copies)
    to_smem = pltpu.make_async_copy(table_all, table, local_sem.at[13])
    to_smem.start()
    to_smem.wait()
    homes = find_owners(table, n_tile, tiles, tuple(me_t * tiles + m for m in range(tiles)))
    owners = [table[me_t, t, SLOT_LANE] // tiles for t in range(tiles)]
    for d in range(n_tile):
        chosen = jnp.int32(0)
        for m in range(tiles):
            chosen = jnp.where(homes[m] == d, m, chosen)
        cot_send[d] = slots[chosen]
    cot_recv[pl.ds(me_t, 1)] = cot_send[pl.ds(me_t, 1)]

    for k in range(1, n_outer):
        straight[k - 1].wait_recv()
        source = lax.rem(outer + n_outer - k, n_outer) * 2 + inner
        forwards.append(
            remote(
                rims.at[source],
                rims.at[source],
                rim_send.at[1, k],
                rim_recv.at[1, k],
                (across, me_c),
            )
        )
    cot_copies = to_tiles(1, lambda d: cot_send.at[d], cot_recv.at[me_t])

    finish(get_own)
    finish(small_copies)
    widen_weights(dot(cw_all[...].reshape(C, C * TAPS), tap_sel[...]), wide)
    down = jnp.zeros((C, 4 * C), F32)
    for c in range(n_chan):
        down = down + dot(dw_all[c], down_sel[c])
    down_t = down.T.astype(BF16)
    down = down.astype(BF16)

    finish(forwards)
    for copy in straight:
        copy.wait_send()
    lane = lax.broadcasted_iota(jnp.int32, (local, 128), 1)
    for t in range(tiles):
        strips = []
        corners = jnp.zeros((local, 128), F32)
        for k in range(4):
            link = table[me_t, t, k]
            chosen = lax.rem(k + 2 + table[me_t, t, 4 + k], 4)
            block = rims[link // tiles, lax.rem(link, tiles)].astype(F32)
            strip = block[:, :S]
            for r in range(1, 4):
                strip = jnp.where(chosen == r, block[:, r * S : r * S + S], strip)
            strips.append(strip)
            link = table[me_t, t, 8 + k]
            chosen = lax.rem(k + 3 + table[me_t, t, 12 + k], 4)
            held = jnp.maximum(link, 0)
            block = rims[held // tiles, lax.rem(held, tiles)].astype(F32)
            value = block[:, :1]
            for r in range(1, 4):
                value = jnp.where(chosen == r, block[:, r * S : r * S + 1], value)
            value = jnp.where(link >= 0, value, jnp.zeros_like(value))
            corners = jnp.where(lane == k, value, corners)
        north, west, south, east = strips
        halos[t] = jnp.concatenate([west, east, north, south, corners], axis=1).astype(BF16)
    halo_all[pl.ds(me_c, 1)] = halos[pl.ds(me_c * per, per)][None]
    halo_copies = to_chans(4, lambda c: halos.at[pl.ds(c * per, per)], halo_all.at[me_c])

    finish(feat_copies)
    for t in range(per):
        pixels = feat_all[:, t].reshape(C, S * S)
        for j in range(8):
            moved = dot(pixels[:, 512 * j : 512 * j + 512], phase_sel[...])
            for p in range(4):
                phases[t, p, :, 128 * j : 128 * j + 128] = moved[:, p * 128 : p * 128 + 128]

    finish(halo_copies)
    bias = jnp.concatenate([cb_all[...].reshape(C, 128)[:, :1]] * 4, axis=0)
    for t in range(per):
        halo = halo_all[:, t].reshape(C, 6 * S)
        sides = dot(halo[:, : 2 * S], side_sel[...])
        caps = dot(halo[:, 2 * S :], cap_sel[...])
        fill_window([phases[t, p] for p in range(4)], sides, caps, window, t)
        pre = dot(wide[...], window[t]) + bias
        pre_act[t] = pre
        hidden[t] = (pre * (1.0 / (1.0 + jnp.exp(-pre)))).astype(BF16)
        quarter[t] = dot(down, hidden[t]).astype(BF16)
    quarter_group[pl.ds(me_c, 1)] = quarter[:, chan_rows(me_c)][None]
    quarter_copies = to_chans(
        5, lambda c: quarter.at[:, chan_rows(c)], quarter_group.at[me_c]
    )

    finish(cot_copies)
    for t in range(tiles):
        cot_group[t] = cot_recv[owners[t]]
    cot_all[pl.ds(me_c, 1)] = cot_group[pl.ds(me_c * per, per)][None]
    cot_chan_copies = to_chans(
        6, lambda c: cot_group.at[pl.ds(c * per, per)], cot_all.at[me_c]
    )

    finish(quarter_copies)
    for d in range(n_tile):
        chosen = jnp.int32(0)
        for t in range(tiles):
            chosen = jnp.where(owners[t] == d, t, chosen)
        quarter_send[d] = quarter_group[chosen // per, lax.rem(chosen, per)]
    quarter_recv[pl.ds(me_t, 1)] = quarter_send[pl.ds(me_t, 1)]
    quarter_copies = to_tiles(2, lambda d: quarter_send.at[d], quarter_recv.at[me_t])

    finish(cot_chan_copies)
    grad_wide = jnp.zeros((4 * C, 16 * C), F32)
    grad_down = jnp.zeros((C, 4 * C), F32)
    grad_bias = jnp.zeros((8, 4 * C), F32)
    ones = jnp.ones((8, QUARTER), BF16)
    for t in range(per):
        back = cot_all[:, t].reshape(C, QUARTER)
        pre = pre_act[t]
        squashed = 1.0 / (1.0 + jnp.exp(-pre))
        slope = squashed * (1.0 + pre * (1.0 - squashed))
        grad_pre = (dot(down_t, back) * slope).astype(BF16)
        grad_down = grad_down + dot_nt(back, hidden[t])
        grad_bias = grad_bias + dot_nt(ones, grad_pre)
        grad_wide = grad_wide + dot_nt(grad_pre, window[t])
    taps = []
    for dy in range(3):
        for dx in range(3):
            total = jnp.zeros((C, C), F32)
            for a in range(2):
                for b in range(2):
                    row = (a * 2 + b) * C
                    col = ((a + dy) * 4 + b + dx) * C
                    total = total + grad_wide[row : row + C, col : col + C]
            taps.append(total)
    pack[:, : TAPS * C] = split_dot_nt(jnp.concatenate(taps, axis=1), tap_sel[...])
    pack[:, TAPS * C :] = jnp.zeros((C, PACK - TAPS * C), F32)
    grad_down = split_dot_nt(grad_down, down_sel[...].reshape(4 * C, 4 * C))
    total = grad_bias[:1, :C]
    for ab in range(1, 4):
        total = total + grad_bias[:1, ab * C : ab * C + C]
    for c in range(n_chan):
        rows = slice(c * local, c * local + local)
        pack[c * local : c * local + 1, BIAS_COL : BIAS_COL + local] = total[:, rows]
        wide_cols = slice(c * 4 * local, (c + 1) * 4 * local)
        for n in range(C // local):
            col = DOWN_COL + n * 4 * local
            pack[rows, col : col + 4 * local] = grad_down[n * local : (n + 1) * local, wide_cols]

    pack_recv[pl.ds(me_c, 1)] = pack[chan_rows(me_c)][None]
    finish(to_chans(7, lambda c: pack.at[chan_rows(c)], pack_recv.at[me_c]))
    total = pack_recv[0]
    for c in range(1, n_chan):
        total = total + pack_recv[c]
    n_pieces = PACK // 128
    if n_tile == n_pieces:
        for n in range(n_pieces):
            pieces[n] = total[:, n * 128 : n * 128 + 128]
        pieces_recv[pl.ds(me_t, 1)] = pieces[pl.ds(me_t, 1)]
        finish(to_tiles(3, lambda d: pieces.at[d], pieces_recv.at[me_t]))
        total = pieces_recv[0]
        for s in range(1, n_tile):
            total = total + pieces_recv[s]
        grads_out[pl.ds(me_t, 1)] = total[None]
        finish(to_tiles(4, lambda d: grads_out.at[me_t], grads_out.at[me_t]))
    else:
        pieces[pl.ds(me_t, 1)] = total[None]
        finish(to_tiles(3, lambda d: pieces.at[me_t], pieces.at[me_t]))
        total = pieces[0]
        for s in range(1, n_tile):
            total = total + pieces[s]
        for n in range(n_pieces):
            grads_out[n] = total[:, n * 128 : n * 128 + 128]

    finish(quarter_copies)
    for m in range(tiles):
        placed_out[m] = quarter_recv[homes[m]]


def finish_kernel(placed, grads, join_sel, coarse, grad_conv, grad_bias, grad_down):
    local = coarse.shape[1]
    for n in range(coarse.shape[0]):
        for j in range(16):
            lanes = slice((j % 8) * 128, (j % 8) * 128 + 128)
            q = n * 4 + (j // 8) * 2
            both = jnp.concatenate([placed[q, :, lanes], placed[q + 1, :, lanes]], axis=1)
            coarse[n, :, 256 * j : 256 * j + 256] = dot(both, join_sel[...]).astype(BF16)
    whole = jnp.concatenate([grads[n] for n in range(grads.shape[0])], axis=1)
    grad_conv[...] = whole[:, : TAPS * C]
    grad_bias[...] = whole[:1, BIAS_COL : BIAS_COL + local]
    for n in range(C // local):
        col = DOWN_COL + n * 4 * local
        grad_down[n * local : (n + 1) * local] = whole[:, col : col + 4 * local]


def on_device(
    n_tile,
    n_chan,
    features,
    conv_weight,
    conv_bias,
    down_weight,
    cotangent,
    edge_links,
    edge_turns,
    corner_links,
    corner_turns,
    child_slot,
):
    tiles, local = features.shape[0], features.shape[1]
    per = tiles // n_chan
    n_pieces = PACK // 128
    hbm = pl.BlockSpec(memory_space=pl.ANY)
    vmem = pl.BlockSpec(memory_space=pltpu.VMEM)
    smem = pl.BlockSpec(memory_space=pltpu.SMEM)
    table = jnp.concatenate(
        [edge_links, edge_turns, corner_links, corner_turns, child_slot[:, None]], axis=1
    )
    table = jnp.pad(table, ((0, 0), (0, 128 - table.shape[1])))

    def const(values):
        return jnp.asarray(values, BF16)

    half = half_selector()
    selectors = [
        const(rim_selector()),
        const(half),
        const(phase_selector()),
        const(side_selector()),
        const(cap_selector()),
        const(tap_selector()),
        const(down_selector(n_chan)),
    ]
    split = n_tile == n_pieces
    piece_shape = (n_tile, local, 128 if split else PACK)
    dma = pltpu.SemaphoreType.DMA
    placed, grads = pl.pallas_call(
        functools.partial(level_kernel, n_tile, n_chan, tiles),
        out_shape=[
            jax.ShapeDtypeStruct((tiles, local, QUARTER), BF16),
            jax.ShapeDtypeStruct((n_pieces, local, 128), F32),
        ],
        in_specs=[hbm] * 12 + [smem],
        out_specs=[vmem] * 2,
        scratch_shapes=[
            pltpu.VMEM(features.shape, BF16),
            pltpu.VMEM(cotangent.shape, BF16),
        ]
        + [pltpu.VMEM(selector.shape, BF16) for selector in selectors]
        + [
            pltpu.VMEM((n_chan, per, local, S * S), BF16),
            pltpu.VMEM((n_chan, local, C * TAPS), BF16),
            pltpu.VMEM((n_chan, C, local * 4), BF16),
            pltpu.VMEM((n_chan, local, 128), F32),
            pltpu.VMEM((n_tile, tiles, 128), jnp.int32),
            pltpu.SMEM((n_tile, tiles, 128), jnp.int32),
            pltpu.VMEM((n_tile, tiles, local, 4 * S), BF16),
            pltpu.VMEM((tiles, local, 6 * S), BF16),
            pltpu.VMEM((n_chan, per, local, 6 * S), BF16),
            pltpu.VMEM((tiles, local, QUARTER), BF16),
            pltpu.VMEM((n_tile, local, QUARTER), BF16),
            pltpu.VMEM((n_tile, local, QUARTER), BF16),
            pltpu.VMEM((tiles, local, QUARTER), BF16),
            pltpu.VMEM((n_chan, per, local, QUARTER), BF16),
            pltpu.VMEM((4 * C, 16 * C), BF16),
            pltpu.VMEM((per, 4, C, QUARTER), F32),
            pltpu.VMEM((per, 16 * C, QUARTER), BF16),
            pltpu.VMEM((per, 4 * C, QUARTER), F32),
            pltpu.VMEM((per, 4 * C, QUARTER), BF16),
            pltpu.VMEM((per, C, QUARTER), BF16),
            pltpu.VMEM((n_chan, per, local, QUARTER), BF16),
            pltpu.VMEM((n_tile, local, QUARTER), BF16),
            pltpu.VMEM((n_tile, local, QUARTER), BF16),
            pltpu.VMEM((C, PACK), F32),
            pltpu.VMEM((n_chan, local, PACK), F32),
            pltpu.VMEM(piece_shape, F32),
            pltpu.VMEM((n_tile, local, 128), F32),
            dma((14,)),
            dma((8, n_chan)),
            dma((8, n_chan)),
            dma((5, n_tile)),
            dma((5, n_tile)),
            dma((2, n_tile // 2)),
            dma((2, n_tile // 2)),
        ],
        compiler_params=pltpu.CompilerParams(
            collective_id=0, has_side_effects=True, vmem_limit_bytes=VMEM_LIMIT
        ),
        name="unet_level",
    )(features, cotangent, conv_weight, down_weight, table, *selectors, conv_bias)
    coarse, grad_conv, grad_bias, grad_down = pl.pallas_call(
        finish_kernel,
        out_shape=[
            jax.ShapeDtypeStruct(cotangent.shape, BF16),
            jax.ShapeDtypeStruct(conv_weight.shape, F32),
            jax.ShapeDtypeStruct((1, local), F32),
            jax.ShapeDtypeStruct(down_weight.shape, F32),
        ],
        in_specs=[vmem] * 3,
        out_specs=[vmem] * 4,
        compiler_params=pltpu.CompilerParams(vmem_limit_bytes=VMEM_LIMIT),
        name="finish",
    )(placed, grads, const(half.T))
    return (coarse, grad_conv, grad_bias.reshape(local), grad_down)


def solution(mesh):
    n_tile, n_chan = mesh.shape["tile"], mesh.shape["chan"]
    in_specs = (
        P("tile", "chan", None),
        P("chan", None),
        P("chan"),
        P(None, "chan"),
        P("tile", "chan", None),
        P("tile", None),
        P("tile", None),
        P("tile", None),
        P("tile", None),
        P("tile"),
    )
    out_specs = (P("tile", "chan", None), P("chan", None), P("chan"), P(None, "chan"))
    return jax.shard_map(
        functools.partial(on_device, n_tile, n_chan),
        mesh=mesh,
        in_specs=in_specs,
        out_specs=out_specs,
        check_vma=False,
    )
```

profile of v0, /device:TPU:0, one launch (start us, length us, event | category | flops | bytes accessed | tf_op | source)
XLA Modules:
  0.0 67.0 jit_solution(10073680183956212076)
XLA Ops:
  0.6 0.8 %copy.22 = s32[8,4]{1,0:T(8,128)S(1)} copy(s32[8,4]{0,1:T(4,128)} %param.23) | data formatting | bytes 256 | tf_op args[5]
  1.4 0.8 %copy.23 = s32[8,4]{1,0:T(8,128)S(1)} copy(s32[8,4]{0,1:T(4,128)} %param.24) | data formatting | bytes 256 | tf_op args[6]
  2.1 0.8 %copy.24 = s32[8,4]{1,0:T(8,128)S(1)} copy(s32[8,4]{0,1:T(4,128)} %param.25) | data formatting | bytes 256 | tf_op args[7]
  2.9 0.8 %copy.25 = s32[8,4]{1,0:T(8,128)S(1)} copy(s32[8,4]{0,1:T(4,128)} %param.26) | data formatting | bytes 256 | tf_op args[8]
  3.7 0.7 %copy.26 = s32[8,1]{1,0:T(8,128)S(1)} copy(s32[8,1]{0,1:T(1,128)} %bitcast.2) | data formatting | bytes 64 | tf_op jit(solution)/shard_map/broadcast_in_dim | solution.py:569
  4.4 0.1 concatenate.3
  4.5 0.0 copy-start
  4.5 1.2 %copy-done = bf16[8,16,4096]{2,1,0:T(8,128)(2,1)S(1)} copy-done((bf16[8,16,4096]{2,1,0:T(8,128)(2,1)S(1)}, bf16[8,16,4096]{2,1,0:T(8,128)(2,1)}, u32[]{:S(2)}) %copy-start) | copy-done | bytes 1048600
  5.7 0.0 copy-start.1
  5.7 1.1 %copy-done.1 = bf16[576,576]{1,0:T(8,128)(2,1)S(1)} copy-done((bf16[576,576]{1,0:T(8,128)(2,1)S(1)}, bf16[576,576]{1,0:T(8,128)(2,1)}, u32[]{:S(2)}) %copy-start.1) | copy-done | bytes 663576
  6.8 0.0 copy-start.2
  6.8 1.0 %copy-done.2 = bf16[256,1024]{1,0:T(8,128)(2,1)S(1)} copy-done((bf16[256,1024]{1,0:T(8,128)(2,1)S(1)}, bf16[256,1024]{1,0:T(8,128)(2,1)}, u32[]{:S(2)}) %copy-start.2) | copy-done | bytes 524312
  7.9 0.0 copy-start.3
  7.9 1.0 %copy-done.3 = bf16[512,512]{1,0:T(8,128)(2,1)S(1)} copy-done((bf16[512,512]{1,0:T(8,128)(2,1)S(1)}, bf16[512,512]{1,0:T(8,128)(2,1)}, u32[]{:S(2)}) %copy-start.3) | copy-done | bytes 524312
  8.9 0.0 copy-start.4
  8.9 0.9 %copy-done.4 = bf16[2,16,4096]{2,1,0:T(8,128)(2,1)S(1)} copy-done((bf16[2,16,4096]{2,1,0:T(8,128)(2,1)S(1)}, bf16[2,16,4096]{2,1,0:T(8,128)(2,1)}, u32[]{:S(2)}) %copy-start.4) | copy-done | bytes 262168
  9.8 0.0 copy-start.6
  9.8 0.9 %copy-done.6 = bf16[4,64,256]{2,1,0:T(8,128)(2,1)S(1)} copy-done((bf16[4,64,256]{2,1,0:T(8,128)(2,1)S(1)}, bf16[4,64,256]{2,1,0:T(8,128)(2,1)}, u32[]{:S(2)}) %copy-start.6) | copy-done | bytes 131096
  10.8 0.0 copy-start.7
  10.8 0.9 %copy-done.7 = bf16[256,256]{1,0:T(8,128)(2,1)S(1)} copy-done((bf16[256,256]{1,0:T(8,128)(2,1)S(1)}, bf16[256,256]{1,0:T(8,128)(2,1)}, u32[]{:S(2)}) %copy-start.7) | copy-done | bytes 131096
  11.7 0.0 copy-start.8
  11.7 0.7 %copy-done.8 = bf16[16,576]{1,0:T(8,128)(2,1)S(1)} copy-done((bf16[16,576]{1,0:T(8,128)(2,1)S(1)}, bf16[16,576]{1,0:T(8,128)(2,1)}, u32[]{:S(2)}) %copy-start.8) | copy-done | bytes 18456
  12.4 0.0 copy-start.9
  12.4 0.7 %copy-done.9 = bf16[64,64]{1,0:T(8,128)(2,1)S(1)} copy-done((bf16[64,64]{1,0:T(8,128)(2,1)S(1)}, bf16[64,64]{1,0:T(8,128)(2,1)}, u32[]{:S(2)}) %copy-start.9) | copy-done | bytes 8216
  13.1 0.0 copy-start.10
  13.1 0.7 copy-done.10
  13.8 0.0 copy-start.5
  13.8 51.9 %unet_level.1 = (bf16[8,16,1024]{2,1,0:T(8,128)(2,1)S(1)}, f32[8,16,128]{2,1,0:T(8,128)S(1)}) custom-call(bf16[8,16,4096]{2,1,0:T(8,128)(2,1)S(1)} %copy-done, bf16[2,16,4096]{2,1,0:T(8,128)(2,1)S(1)} %copy-done.4, bf16[16,576]{1,0:T(8,128)(2,1)S(1)} %copy-done.8, bf16[64,64]{1,0:T(8,128)(2,1)S(1)} %copy-done.9, s32[8,128]{1,0:T(8,128)S(1)} %pad.4.table_hbm, ...), custom_call_target="tpu_custom_call" | custom-call | tf_op jit(solution)/shard_map/unet_level/pallas_call | solution.py:589
  65.6 0.0 copy-done.5
  65.6 1.4 %finish.1 = (bf16[2,16,4096]{2,1,0:T(8,128)(2,1)}, f32[16,576]{1,0:T(8,128)}, f32[1,16]{1,0:T(1,128)}, f32[64,64]{1,0:T(8,128)}) custom-call(bf16[8,16,1024]{2,1,0:T(8,128)(2,1)S(1)} %get-tuple-element.10.placed, f32[8,16,128]{2,1,0:T(8,128)S(1)} %get-tuple-element.11.grads, bf16[256,256]{1,0:T(8,128)(2,1)S(1)} %copy-done.5), custom_call_target="tpu_custom_call" | custom-call | tf_op jit(solution)/shard_map/finish/pallas_call | solution.py:643
  (1 shorter events, 0.0 us)
Async XLA Ops:
  4.5 1.2 %copy-start = (bf16[8,16,4096]{2,1,0:T(8,128)(2,1)S(1)}, bf16[8,16,4096]{2,1,0:T(8,128)(2,1)}, u32[]{:S(2)}) copy-start(bf16[8,16,4096]{2,1,0:T(8,128)(2,1)} %feat_hbm.1) | copy-start | bytes 3145732
  5.7 1.1 %copy-start.1 = (bf16[576,576]{1,0:T(8,128)(2,1)S(1)}, bf16[576,576]{1,0:T(8,128)(2,1)}, u32[]{:S(2)}) copy-start(bf16[576,576]{1,0:T(8,128)(2,1)} %constant.23.clone.tap_sel_hbm) | copy-start | bytes 1990660
  6.8 1.0 %copy-start.2 = (bf16[256,1024]{1,0:T(8,128)(2,1)S(1)}, bf16[256,1024]{1,0:T(8,128)(2,1)}, u32[]{:S(2)}) copy-start(bf16[256,1024]{1,0:T(8,128)(2,1)} %constant.22.clone.cap_sel_hbm) | copy-start | bytes 1572868
  7.9 1.0 %copy-start.3 = (bf16[512,512]{1,0:T(8,128)(2,1)S(1)}, bf16[512,512]{1,0:T(8,128)(2,1)}, u32[]{:S(2)}) copy-start(bf16[512,512]{1,0:T(8,128)(2,1)} %constant.20.clone.phase_sel_hbm) | copy-start | bytes 1572868
  8.9 0.9 %copy-start.4 = (bf16[2,16,4096]{2,1,0:T(8,128)(2,1)S(1)}, bf16[2,16,4096]{2,1,0:T(8,128)(2,1)}, u32[]{:S(2)}) copy-start(bf16[2,16,4096]{2,1,0:T(8,128)(2,1)} %cot_hbm.1) | copy-start | bytes 786436
  9.8 0.9 %copy-start.6 = (bf16[4,64,256]{2,1,0:T(8,128)(2,1)S(1)}, bf16[4,64,256]{2,1,0:T(8,128)(2,1)}, u32[]{:S(2)}) copy-start(bf16[4,64,256]{2,1,0:T(8,128)(2,1)} %constant.24.clone.down_sel_hbm) | copy-start | bytes 393220
  10.8 0.9 %copy-start.7 = (bf16[256,256]{1,0:T(8,128)(2,1)S(1)}, bf16[256,256]{1,0:T(8,128)(2,1)}, u32[]{:S(2)}) copy-start(bf16[256,256]{1,0:T(8,128)(2,1)} %constant.19.clone.half_sel_hbm) | copy-start | bytes 393220
  11.7 0.7 %copy-start.8 = (bf16[16,576]{1,0:T(8,128)(2,1)S(1)}, bf16[16,576]{1,0:T(8,128)(2,1)}, u32[]{:S(2)}) copy-start(bf16[16,576]{1,0:T(8,128)(2,1)} %cw_hbm.1) | copy-start | bytes 55300
  12.4 0.7 %copy-start.9 = (bf16[64,64]{1,0:T(8,128)(2,1)S(1)}, bf16[64,64]{1,0:T(8,128)(2,1)}, u32[]{:S(2)}) copy-start(bf16[64,64]{1,0:T(8,128)(2,1)} %dw_hbm.1) | copy-start | bytes 24580
  13.1 0.7 copy-start.10
  13.8 51.9 %copy-start.5 = (bf16[256,256]{1,0:T(8,128)(2,1)S(1)}, bf16[256,256]{1,0:T(8,128)(2,1)}, u32[]{:S(2)}) copy-start(bf16[256,256]{1,0:T(8,128)(2,1)} %constant.25.clone.join_sel) | copy-start | bytes 393220
where the time goes:
time: 67.6 us; the launch traced here: 67 us
  Pallas kernels  53.2 us (79%)
  local copies, waits for them, and re-layouts  13.1 us (19%)
    pallas_call x1, Pallas kernels, on_device(): pl.pallas_call(functools.partial(level_kernel, n_tile, n_chan, tiles), ou...  51.9 us
    unnamed x26, local copies, waits for them, and re-layouts  12.3 us
    pallas_call x1, Pallas kernels, on_device(): pl.pallas_call(finish_kernel, out_shape=[jax.ShapeDtypeStruct(cotangent.s...  1.37 us

commit v1 on v0

--- a/solution.py
+++ b/solution.py
@@ -16,11 +16,11 @@
 MESH = pl.DeviceIdType.MESH
 F32 = jnp.float32
 BF16 = jnp.bfloat16
-VMEM_LIMIT = 50 * 1024 * 1024
+VMEM_LIMIT = 63 * 1024 * 1024
 PACK = 1024
+FEAT = 8
 BIAS_COL = TAPS * C
 DOWN_COL = BIAS_COL + C
-SLOT_LANE = 16
 
 
 def rim_selector():
@@ -130,7 +130,7 @@
 def find_owners(table, groups, tiles, wanted):
     def step(s, found):
         for t in range(tiles):
-            value = table[s, t, SLOT_LANE]
+            value = table[s, t, 0]
             found = tuple(jnp.where(value == w, s, f) for w, f in zip(wanted, found))
         return found
 
@@ -195,7 +195,6 @@
     cot_hbm,
     cw_hbm,
     dw_hbm,
-    table_hbm,
     rim_sel_hbm,
     half_sel_hbm,
     phase_sel_hbm,
@@ -204,6 +203,11 @@
     tap_sel_hbm,
     down_sel_hbm,
     cb_smem,
+    el_smem,
+    et_smem,
+    cl_smem,
+    ct_smem,
+    slot_smem,
     placed_out,
     grads_out,
     feat,
@@ -232,7 +236,7 @@
     wide,
     phases,
     window,
-    pre_act,
+    slope,
     hidden,
     quarter,
     quarter_group,
@@ -268,11 +272,10 @@
     get_rim_sel = fetch(rim_sel_hbm, rim_sel, 1)
     get_cot = fetch(cot_hbm, cot, 2)
     get_half_sel = fetch(half_sel_hbm, half_sel, 3)
-    get_table = fetch(table_hbm, table_all.at[me_t], 4)
     get_own = [
         fetch(cw_hbm, cw_all.at[me_c], 5),
         fetch(dw_hbm, dw_all.at[me_c], 6),
-        fetch(feat_hbm.at[pl.ds(me_c * per, per)], feat_all.at[me_c], 7),
+        fetch(feat_hbm.at[pl.ds(me_c * per, per)], feat_all.at[me_c], 4),
         fetch(phase_sel_hbm, phase_sel, 8),
         fetch(side_sel_hbm, side_sel, 9),
         fetch(cap_sel_hbm, cap_sel, 10),
@@ -284,13 +287,17 @@
     for n in range(local):
         bias = jnp.where(row == n, cb_smem[n], bias)
     cb_all[pl.ds(me_c, 1)] = bias[None]
+    row = lax.broadcasted_iota(jnp.int32, (tiles, 128), 0)
+    own_slots = jnp.zeros((tiles, 128), jnp.int32)
+    for t in range(tiles):
+        own_slots = jnp.where(row == t, slot_smem[0, t], own_slots)
+    table_all[pl.ds(me_t, 1)] = own_slots[None]
 
     get_feat.wait()
     get_rim_sel.wait()
     pixels = feat[...].reshape(tiles * local, S * S)
     my_rims = dot(pixels, rim_sel[...]).astype(BF16)
     rims[pl.ds(me_t, 1)] = my_rims.reshape(1, tiles, local, 4 * S)
-    get_table.wait()
 
     pl.semaphore_wait(pltpu.get_barrier_semaphore(), n_tile - 1 + n_chan - 1)
 
@@ -341,7 +348,10 @@
         + to_chans(2, lambda c: dw_hbm, dw_all.at[me_c])
         + to_chans(3, lambda c: cb_all.at[me_c], cb_all.at[me_c])
     )
-    feat_copies = to_chans(0, lambda c: feat_hbm.at[pl.ds(c * per, per)], feat_all.at[me_c])
+    feat_copies = [
+        to_chans(FEAT + t, lambda c: feat_hbm.at[c * per + t], feat_all.at[me_c, t])
+        for t in range(per)
+    ]
 
     get_cot.wait()
     get_half_sel.wait()
@@ -356,11 +366,11 @@
             slots[n * 4 + (j // 8) * 2 + 1, :, lanes] = rows[:, 128:]
 
     finish(table_copies)
-    to_smem = pltpu.make_async_copy(table_all, table, local_sem.at[13])
+    to_smem = pltpu.make_async_copy(table_all, table, local_sem.at[7])
     to_smem.start()
     to_smem.wait()
     homes = find_owners(table, n_tile, tiles, tuple(me_t * tiles + m for m in range(tiles)))
-    owners = [table[me_t, t, SLOT_LANE] // tiles for t in range(tiles)]
+    owners = [slot_smem[0, t] // tiles for t in range(tiles)]
     for d in range(n_tile):
         chosen = jnp.int32(0)
         for m in range(tiles):
@@ -391,6 +401,15 @@
     down_t = down.T.astype(BF16)
     down = down.astype(BF16)
 
+    def deinterleave(t):
+        finish(feat_copies[t])
+        pixels = feat_all[:, t].reshape(C, S * S)
+        for j in range(8):
+            moved = dot(pixels[:, 512 * j : 512 * j + 512], phase_sel[...])
+            for p in range(4):
+                phases[t, p, :, 128 * j : 128 * j + 128] = moved[:, p * 128 : p * 128 + 128]
+
+    deinterleave(0)
     finish(forwards)
     for copy in straight:
         copy.wait_send()
@@ -399,15 +418,15 @@
         strips = []
         corners = jnp.zeros((local, 128), F32)
         for k in range(4):
-            link = table[me_t, t, k]
-            chosen = lax.rem(k + 2 + table[me_t, t, 4 + k], 4)
+            link = el_smem[k, t]
+            chosen = lax.rem(k + 2 + et_smem[k, t], 4)
             block = rims[link // tiles, lax.rem(link, tiles)].astype(F32)
             strip = block[:, :S]
             for r in range(1, 4):
                 strip = jnp.where(chosen == r, block[:, r * S : r * S + S], strip)
             strips.append(strip)
-            link = table[me_t, t, 8 + k]
-            chosen = lax.rem(k + 3 + table[me_t, t, 12 + k], 4)
+            link = cl_smem[k, t]
+            chosen = lax.rem(k + 3 + ct_smem[k, t], 4)
             held = jnp.maximum(link, 0)
             block = rims[held // tiles, lax.rem(held, tiles)].astype(F32)
             value = block[:, :1]
@@ -420,30 +439,6 @@
     halo_all[pl.ds(me_c, 1)] = halos[pl.ds(me_c * per, per)][None]
     halo_copies = to_chans(4, lambda c: halos.at[pl.ds(c * per, per)], halo_all.at[me_c])
 
-    finish(feat_copies)
-    for t in range(per):
-        pixels = feat_all[:, t].reshape(C, S * S)
-        for j in range(8):
-            moved = dot(pixels[:, 512 * j : 512 * j + 512], phase_sel[...])
-            for p in range(4):
-                phases[t, p, :, 128 * j : 128 * j + 128] = moved[:, p * 128 : p * 128 + 128]
-
-    finish(halo_copies)
-    bias = jnp.concatenate([cb_all[...].reshape(C, 128)[:, :1]] * 4, axis=0)
-    for t in range(per):
-        halo = halo_all[:, t].reshape(C, 6 * S)
-        sides = dot(halo[:, : 2 * S], side_sel[...])
-        caps = dot(halo[:, 2 * S :], cap_sel[...])
-        fill_window([phases[t, p] for p in range(4)], sides, caps, window, t)
-        pre = dot(wide[...], window[t]) + bias
-        pre_act[t] = pre
-        hidden[t] = (pre * (1.0 / (1.0 + jnp.exp(-pre)))).astype(BF16)
-        quarter[t] = dot(down, hidden[t]).astype(BF16)
-    quarter_group[pl.ds(me_c, 1)] = quarter[:, chan_rows(me_c)][None]
-    quarter_copies = to_chans(
-        5, lambda c: quarter.at[:, chan_rows(c)], quarter_group.at[me_c]
-    )
-
     finish(cot_copies)
     for t in range(tiles):
         cot_group[t] = cot_recv[owners[t]]
@@ -451,6 +446,26 @@
     cot_chan_copies = to_chans(
         6, lambda c: cot_group.at[pl.ds(c * per, per)], cot_all.at[me_c]
     )
+
+    for t in range(1, per):
+        deinterleave(t)
+    finish(halo_copies)
+    bias = jnp.concatenate([cb_all[...].reshape(C, 128)[:, :1]] * 4, axis=0)
+    quarter_copies = []
+    for t in range(per):
+        halo = halo_all[:, t].reshape(C, 6 * S)
+        sides = dot(halo[:, : 2 * S], side_sel[...])
+        caps = dot(halo[:, 2 * S :], cap_sel[...])
+        fill_window([phases[t, p] for p in range(4)], sides, caps, window, t)
+        pre = dot(wide[...], window[t]) + bias
+        squashed = 1.0 / (1.0 + jnp.exp(-pre))
+        slope[t] = squashed * (1.0 + pre * (1.0 - squashed))
+        hidden[t] = (pre * squashed).astype(BF16)
+        quarter[t] = dot(down, hidden[t]).astype(BF16)
+        quarter_group[pl.ds(me_c, 1), t] = quarter[t, chan_rows(me_c)][None]
+        quarter_copies += to_chans(
+            FEAT + per + t, lambda c: quarter.at[t, chan_rows(c)], quarter_group.at[me_c, t]
+        )
 
     finish(quarter_copies)
     for d in range(n_tile):
@@ -468,10 +483,7 @@
     ones = jnp.ones((8, QUARTER), BF16)
     for t in range(per):
         back = cot_all[:, t].reshape(C, QUARTER)
-        pre = pre_act[t]
-        squashed = 1.0 / (1.0 + jnp.exp(-pre))
-        slope = squashed * (1.0 + pre * (1.0 - squashed))
-        grad_pre = (dot(down_t, back) * slope).astype(BF16)
+        grad_pre = (dot(down_t, back) * slope[t]).astype(BF16)
         grad_down = grad_down + dot_nt(back, hidden[t])
         grad_bias = grad_bias + dot_nt(ones, grad_pre)
         grad_wide = grad_wide + dot_nt(grad_pre, window[t])
@@ -562,13 +574,10 @@
     tiles, local = features.shape[0], features.shape[1]
     per = tiles // n_chan
     n_pieces = PACK // 128
-    hbm = pl.BlockSpec(memory_space=pl.ANY)
+    hbm = pl.BlockSpec(memory_space=pltpu.HBM)
     vmem = pl.BlockSpec(memory_space=pltpu.VMEM)
     smem = pl.BlockSpec(memory_space=pltpu.SMEM)
-    table = jnp.concatenate(
-        [edge_links, edge_turns, corner_links, corner_turns, child_slot[:, None]], axis=1
-    )
-    table = jnp.pad(table, ((0, 0), (0, 128 - table.shape[1])))
+    tables = [edge_links.T, edge_turns.T, corner_links.T, corner_turns.T, child_slot[None]]
 
     def const(values):
         return jnp.asarray(values, BF16)
@@ -592,7 +601,7 @@
             jax.ShapeDtypeStruct((tiles, local, QUARTER), BF16),
             jax.ShapeDtypeStruct((n_pieces, local, 128), F32),
         ],
-        in_specs=[hbm] * 12 + [smem],
+        in_specs=[hbm] * 11 + [smem] * 6,
         out_specs=[vmem] * 2,
         scratch_shapes=[
             pltpu.VMEM(features.shape, BF16),
@@ -627,9 +636,9 @@
             pltpu.VMEM((n_chan, local, PACK), F32),
             pltpu.VMEM(piece_shape, F32),
             pltpu.VMEM((n_tile, local, 128), F32),
-            dma((14,)),
-            dma((8, n_chan)),
-            dma((8, n_chan)),
+            dma((13,)),
+            dma((FEAT + 2 * per, n_chan)),
+            dma((FEAT + 2 * per, n_chan)),
             dma((5, n_tile)),
             dma((5, n_tile)),
             dma((2, n_tile // 2)),
@@ -639,7 +648,7 @@
             collective_id=0, has_side_effects=True, vmem_limit_bytes=VMEM_LIMIT
         ),
         name="unet_level",
-    )(features, cotangent, conv_weight, down_weight, table, *selectors, conv_bias)
+    )(features, cotangent, conv_weight, down_weight, *selectors, conv_bias, *tables)
     coarse, grad_conv, grad_bias, grad_down = pl.pallas_call(
         finish_kernel,
         out_shape=[

time: 67.6 us -> 52.7 us (0.78)
  local copies, waits for them, and re-layouts: 13.1 us -> 0 us
  Pallas kernels: 53.2 us -> 51.9 us
    unnamed x26 -> x0, local copies, waits for them, and re-layouts: 12.3 us -> none
    pallas_call x1, Pallas kernels: 51.9 us -> 49.5 us  [on_device(): pl.pallas_call(functools.partial(level_kernel, n_tile, n_chan, tiles), ou...]
    pallas_call x1, Pallas kernels: 1.37 us -> 2.39 us  [on_device(): pl.pallas_call(finish_kernel, out_shape=[jax.ShapeDtypeStruct(cotangent.s...]
    broadcast_in_dim x1 -> x0, local copies, waits for them, and re-layouts: 0.73 us -> none  [on_device(): child_slot[:, None]]
where the time goes in v1:
time: 52.7 us; the launch traced here: 52.5 us
  Pallas kernels  51.9 us (98%)
  between operations  0.64 us (1%)
    pallas_call x1, Pallas kernels, on_device(): pl.pallas_call(functools.partial(level_kernel, n_tile, n_chan, tiles), ou...  49.5 us
    pallas_call x1, Pallas kernels, on_device(): pl.pallas_call(finish_kernel, out_shape=[jax.ShapeDtypeStruct(cotangent.s...  2.39 us

profile of v1, /device:TPU:0, one launch (start us, length us, event | category | flops | bytes accessed | tf_op | source)
XLA Modules:
  0.0 52.5 jit_solution(264868347074539295)
XLA Ops:
  0.6 49.5 %unet_level.1 = (bf16[8,16,1024]{2,1,0:T(8,128)(2,1)}, f32[8,16,128]{2,1,0:T(8,128)}) custom-call(bf16[8,16,4096]{2,1,0:T(8,128)(2,1)} %feat_hbm.1, bf16[2,16,4096]{2,1,0:T(8,128)(2,1)} %cot_hbm.1, bf16[16,576]{1,0:T(8,128)(2,1)} %cw_hbm.1, bf16[64,64]{1,0:T(8,128)(2,1)} %dw_hbm.1, bf16[4096,256]{1,0:T(8,128)(2,1)} %constant.16.clone.rim_sel_hbm, ...), custom_call_target="tpu_custom_call" | custom-call | tf_op jit(solution)/shard_map/unet_level/pallas_call | solution.py:598
  50.1 2.4 %finish.1 = (bf16[2,16,4096]{2,1,0:T(8,128)(2,1)}, f32[16,576]{1,0:T(8,128)}, f32[1,16]{1,0:T(1,128)}, f32[64,64]{1,0:T(8,128)}) custom-call(bf16[8,16,1024]{2,1,0:T(8,128)(2,1)} %get-tuple-element.10.placed, f32[8,16,128]{2,1,0:T(8,128)} %get-tuple-element.11.grads, bf16[256,256]{1,0:T(8,128)(2,1)} %constant.23.clone.join_sel), custom_call_target="tpu_custom_call" | custom-call | tf_op jit(solution)/shard_map/finish/pallas_call | solution.py:652

commit v2 on v1

--- a/solution.py
+++ b/solution.py
@@ -101,7 +101,9 @@
     rest = a - high.astype(F32)
     middle = rest.astype(BF16)
     low = (rest - middle.astype(F32)).astype(BF16)
-    return dot_nt(high, selector) + dot_nt(middle, selector) + dot_nt(low, selector)
+    rows = a.shape[0]
+    moved = dot_nt(jnp.concatenate([high, middle, low], axis=0), selector)
+    return moved[:rows] + moved[rows : 2 * rows] + moved[2 * rows :]
 
 
 def greet(n_tile, n_chan, me_t, me_c):
@@ -293,12 +295,6 @@
         own_slots = jnp.where(row == t, slot_smem[0, t], own_slots)
     table_all[pl.ds(me_t, 1)] = own_slots[None]
 
-    get_feat.wait()
-    get_rim_sel.wait()
-    pixels = feat[...].reshape(tiles * local, S * S)
-    my_rims = dot(pixels, rim_sel[...]).astype(BF16)
-    rims[pl.ds(me_t, 1)] = my_rims.reshape(1, tiles, local, 4 * S)
-
     pl.semaphore_wait(pltpu.get_barrier_semaphore(), n_tile - 1 + n_chan - 1)
 
     def to_tiles(kind, src, dst):
@@ -331,6 +327,21 @@
         return pl.ds(pl.multiple_of(c * local, local), local)
 
     table_copies = to_tiles(0, lambda d: table_all.at[me_t], table_all.at[me_t])
+    small_copies = (
+        to_chans(1, lambda c: cw_hbm, cw_all.at[me_c])
+        + to_chans(2, lambda c: dw_hbm, dw_all.at[me_c])
+        + to_chans(3, lambda c: cb_all.at[me_c], cb_all.at[me_c])
+    )
+    feat_copies = [
+        to_chans(FEAT + t, lambda c: feat_hbm.at[c * per + t], feat_all.at[me_c, t])
+        for t in range(per)
+    ]
+
+    get_feat.wait()
+    get_rim_sel.wait()
+    pixels = feat[...].reshape(tiles * local, S * S)
+    my_rims = dot(pixels, rim_sel[...]).astype(BF16)
+    rims[pl.ds(me_t, 1)] = my_rims.reshape(1, tiles, local, 4 * S)
     across = outer * 2 + 1 - inner
     forwards = [
         remote(
@@ -343,25 +354,18 @@
         straight.append(
             remote(rims.at[me_t], rims.at[me_t], rim_send.at[0, k], rim_recv.at[0, k], (d, me_c))
         )
-    small_copies = (
-        to_chans(1, lambda c: cw_hbm, cw_all.at[me_c])
-        + to_chans(2, lambda c: dw_hbm, dw_all.at[me_c])
-        + to_chans(3, lambda c: cb_all.at[me_c], cb_all.at[me_c])
-    )
-    feat_copies = [
-        to_chans(FEAT + t, lambda c: feat_hbm.at[c * per + t], feat_all.at[me_c, t])
-        for t in range(per)
-    ]
 
     get_cot.wait()
     get_half_sel.wait()
     coarse_tiles = cot.shape[0]
     cots = cot[...].reshape(coarse_tiles * local, S * S)
+    chunks = [cots[:, 256 * j : 256 * j + 256] for j in range(16)]
+    moved = dot(jnp.concatenate(chunks, axis=0), half_sel[...]).astype(BF16)
     for j in range(16):
-        moved = dot(cots[:, 256 * j : 256 * j + 256], half_sel[...]).astype(BF16)
         lanes = slice((j % 8) * 128, (j % 8) * 128 + 128)
         for n in range(coarse_tiles):
-            rows = moved[n * local : (n + 1) * local]
+            first = (j * coarse_tiles + n) * local
+            rows = moved[first : first + local]
             slots[n * 4 + (j // 8) * 2, :, lanes] = rows[:, :128]
             slots[n * 4 + (j // 8) * 2 + 1, :, lanes] = rows[:, 128:]
 
@@ -404,10 +408,12 @@
     def deinterleave(t):
         finish(feat_copies[t])
         pixels = feat_all[:, t].reshape(C, S * S)
+        chunks = [pixels[:, 512 * j : 512 * j + 512] for j in range(8)]
+        moved = dot(jnp.concatenate(chunks, axis=0), phase_sel[...])
         for j in range(8):
-            moved = dot(pixels[:, 512 * j : 512 * j + 512], phase_sel[...])
+            rows = moved[j * C : (j + 1) * C]
             for p in range(4):
-                phases[t, p, :, 128 * j : 128 * j + 128] = moved[:, p * 128 : p * 128 + 128]
+                phases[t, p, :, 128 * j : 128 * j + 128] = rows[:, p * 128 : p * 128 + 128]
 
     deinterleave(0)
     finish(forwards)
@@ -415,27 +421,27 @@
         copy.wait_send()
     lane = lax.broadcasted_iota(jnp.int32, (local, 128), 1)
     for t in range(tiles):
+        def half_of(link, rim):
+            block = rims[link // tiles, lax.rem(link, tiles)].astype(F32)
+            return jnp.where(rim >= 2, block[:, 128:], block[:, :128])
+
         strips = []
         corners = jnp.zeros((local, 128), F32)
-        for k in range(4):
-            link = el_smem[k, t]
-            chosen = lax.rem(k + 2 + et_smem[k, t], 4)
-            block = rims[link // tiles, lax.rem(link, tiles)].astype(F32)
-            strip = block[:, :S]
-            for r in range(1, 4):
-                strip = jnp.where(chosen == r, block[:, r * S : r * S + S], strip)
-            strips.append(strip)
+        for k, place in enumerate((0, 0, 1, 1)):
+            rim = lax.rem(k + 2 + et_smem[k, t], 4)
+            held = half_of(el_smem[k, t], rim)
+            strips.append(jnp.where(lax.rem(rim, 2) == place, held, pltpu.roll(held, S, 1)))
             link = cl_smem[k, t]
-            chosen = lax.rem(k + 3 + ct_smem[k, t], 4)
-            held = jnp.maximum(link, 0)
-            block = rims[held // tiles, lax.rem(held, tiles)].astype(F32)
-            value = block[:, :1]
-            for r in range(1, 4):
-                value = jnp.where(chosen == r, block[:, r * S : r * S + 1], value)
+            rim = lax.rem(k + 3 + ct_smem[k, t], 4)
+            held = half_of(jnp.maximum(link, 0), rim)
+            near, far = held if k == 0 else pltpu.roll(held, k, 1), pltpu.roll(held, S + k, 1)
+            value = jnp.where(lax.rem(rim, 2) == 0, near, far)
             value = jnp.where(link >= 0, value, jnp.zeros_like(value))
             corners = jnp.where(lane == k, value, corners)
         north, west, south, east = strips
-        halos[t] = jnp.concatenate([west, east, north, south, corners], axis=1).astype(BF16)
+        west_east = jnp.where(lane < S, west, east)
+        north_south = jnp.where(lane < S, north, south)
+        halos[t] = jnp.concatenate([west_east, north_south, corners], axis=1).astype(BF16)
     halo_all[pl.ds(me_c, 1)] = halos[pl.ds(me_c * per, per)][None]
     halo_copies = to_chans(4, lambda c: halos.at[pl.ds(c * per, per)], halo_all.at[me_c])
 
@@ -452,11 +458,12 @@
     finish(halo_copies)
     bias = jnp.concatenate([cb_all[...].reshape(C, 128)[:, :1]] * 4, axis=0)
     quarter_copies = []
+    halo = jnp.concatenate([halo_all[:, t].reshape(C, 6 * S) for t in range(per)], axis=0)
+    sides = dot(halo[:, : 2 * S], side_sel[...])
+    caps = dot(halo[:, 2 * S :], cap_sel[...])
     for t in range(per):
-        halo = halo_all[:, t].reshape(C, 6 * S)
-        sides = dot(halo[:, : 2 * S], side_sel[...])
-        caps = dot(halo[:, 2 * S :], cap_sel[...])
-        fill_window([phases[t, p] for p in range(4)], sides, caps, window, t)
+        rows = slice(t * C, (t + 1) * C)
+        fill_window([phases[t, p] for p in range(4)], sides[rows], caps[rows], window, t)
         pre = dot(wide[...], window[t]) + bias
         squashed = 1.0 / (1.0 + jnp.exp(-pre))
         slope[t] = squashed * (1.0 + pre * (1.0 - squashed))
@@ -543,12 +550,17 @@
 
 def finish_kernel(placed, grads, join_sel, coarse, grad_conv, grad_bias, grad_down):
     local = coarse.shape[1]
+    chunks = []
     for n in range(coarse.shape[0]):
         for j in range(16):
             lanes = slice((j % 8) * 128, (j % 8) * 128 + 128)
             q = n * 4 + (j // 8) * 2
-            both = jnp.concatenate([placed[q, :, lanes], placed[q + 1, :, lanes]], axis=1)
-            coarse[n, :, 256 * j : 256 * j + 256] = dot(both, join_sel[...]).astype(BF16)
+            chunks.append(jnp.concatenate([placed[q, :, lanes], placed[q + 1, :, lanes]], axis=1))
+    moved = dot(jnp.concatenate(chunks, axis=0), join_sel[...]).astype(BF16)
+    for n in range(coarse.shape[0]):
+        for j in range(16):
+            first = (n * 16 + j) * local
+            coarse[n, :, 256 * j : 256 * j + 256] = moved[first : first + local]
     whole = jnp.concatenate([grads[n] for n in range(grads.shape[0])], axis=1)
     grad_conv[...] = whole[:, : TAPS * C]
     grad_bias[...] = whole[:1, BIAS_COL : BIAS_COL + local]

time: 52.7 us -> 52 us (0.987)
  Pallas kernels: 51.9 us -> 51.2 us
where the time goes in v2:
time: 52 us; the launch traced here: 51.8 us
  Pallas kernels  51.2 us (98%)
  between operations  0.64 us (1%)
    pallas_call x1, Pallas kernels, on_device(): pl.pallas_call(functools.partial(level_kernel, n_tile, n_chan, tiles), ou...  49.2 us
    pallas_call x1, Pallas kernels, on_device(): pl.pallas_call(finish_kernel, out_shape=[jax.ShapeDtypeStruct(cotangent.s...  1.96 us

profile of v2, /device:TPU:0, one launch (start us, length us, event | category | flops | bytes accessed | tf_op | source)
XLA Modules:
  0.0 51.8 jit_solution(9011522639278893156)
XLA Ops:
  0.6 49.2 %unet_level.1 = (bf16[8,16,1024]{2,1,0:T(8,128)(2,1)}, f32[8,16,128]{2,1,0:T(8,128)}) custom-call(bf16[8,16,4096]{2,1,0:T(8,128)(2,1)} %feat_hbm.1, bf16[2,16,4096]{2,1,0:T(8,128)(2,1)} %cot_hbm.1, bf16[16,576]{1,0:T(8,128)(2,1)} %cw_hbm.1, bf16[64,64]{1,0:T(8,128)(2,1)} %dw_hbm.1, bf16[4096,256]{1,0:T(8,128)(2,1)} %constant.16.clone.rim_sel_hbm, ...), custom_call_target="tpu_custom_call" | custom-call | tf_op jit(solution)/shard_map/unet_level/pallas_call | solution.py:610
  49.9 2.0 %finish.1 = (bf16[2,16,4096]{2,1,0:T(8,128)(2,1)}, f32[16,576]{1,0:T(8,128)}, f32[1,16]{1,0:T(1,128)}, f32[64,64]{1,0:T(8,128)}) custom-call(bf16[8,16,1024]{2,1,0:T(8,128)(2,1)} %get-tuple-element.10.placed, f32[8,16,128]{2,1,0:T(8,128)} %get-tuple-element.11.grads, bf16[256,256]{1,0:T(8,128)(2,1)} %constant.23.clone.join_sel), custom_call_target="tpu_custom_call" | custom-call | tf_op jit(solution)/shard_map/finish/pallas_call | solution.py:664

commit v3 on v2

--- a/solution.py
+++ b/solution.py
@@ -210,7 +210,7 @@
     cl_smem,
     ct_smem,
     slot_smem,
-    placed_out,
+    coarse_out,
     grads_out,
     feat,
     cot,
@@ -445,18 +445,19 @@
     halo_all[pl.ds(me_c, 1)] = halos[pl.ds(me_c * per, per)][None]
     halo_copies = to_chans(4, lambda c: halos.at[pl.ds(c * per, per)], halo_all.at[me_c])
 
-    finish(cot_copies)
-    for t in range(tiles):
-        cot_group[t] = cot_recv[owners[t]]
-    cot_all[pl.ds(me_c, 1)] = cot_group[pl.ds(me_c * per, per)][None]
-    cot_chan_copies = to_chans(
-        6, lambda c: cot_group.at[pl.ds(c * per, per)], cot_all.at[me_c]
-    )
-
     for t in range(1, per):
         deinterleave(t)
     finish(halo_copies)
     bias = jnp.concatenate([cb_all[...].reshape(C, 128)[:, :1]] * 4, axis=0)
+    def forward_cotangent():
+        finish(cot_copies)
+        for t in range(tiles):
+            cot_group[t] = cot_recv[owners[t]]
+        cot_all[pl.ds(me_c, 1)] = cot_group[pl.ds(me_c * per, per)][None]
+        return to_chans(
+            6, lambda c: cot_group.at[pl.ds(c * per, per)], cot_all.at[me_c]
+        )
+
     quarter_copies = []
     halo = jnp.concatenate([halo_all[:, t].reshape(C, 6 * S) for t in range(per)], axis=0)
     sides = dot(halo[:, : 2 * S], side_sel[...])
@@ -473,15 +474,18 @@
         quarter_copies += to_chans(
             FEAT + per + t, lambda c: quarter.at[t, chan_rows(c)], quarter_group.at[me_c, t]
         )
-
-    finish(quarter_copies)
-    for d in range(n_tile):
-        chosen = jnp.int32(0)
-        for t in range(tiles):
-            chosen = jnp.where(owners[t] == d, t, chosen)
-        quarter_send[d] = quarter_group[chosen // per, lax.rem(chosen, per)]
-    quarter_recv[pl.ds(me_t, 1)] = quarter_send[pl.ds(me_t, 1)]
-    quarter_copies = to_tiles(2, lambda d: quarter_send.at[d], quarter_recv.at[me_t])
+        if t == 0:
+            cot_chan_copies = forward_cotangent()
+
+    def forward_quarters():
+        finish(quarter_copies)
+        for d in range(n_tile):
+            chosen = jnp.int32(0)
+            for t in range(tiles):
+                chosen = jnp.where(owners[t] == d, t, chosen)
+            quarter_send[d] = quarter_group[chosen // per, lax.rem(chosen, per)]
+        quarter_recv[pl.ds(me_t, 1)] = quarter_send[pl.ds(me_t, 1)]
+        return to_tiles(2, lambda d: quarter_send.at[d], quarter_recv.at[me_t])
 
     finish(cot_chan_copies)
     grad_wide = jnp.zeros((4 * C, 16 * C), F32)
@@ -494,6 +498,8 @@
         grad_down = grad_down + dot_nt(back, hidden[t])
         grad_bias = grad_bias + dot_nt(ones, grad_pre)
         grad_wide = grad_wide + dot_nt(grad_pre, window[t])
+        if t == 0:
+            quarter_moves = forward_quarters()
     taps = []
     for dy in range(3):
         for dx in range(3):
@@ -518,6 +524,21 @@
             col = DOWN_COL + n * 4 * local
             pack[rows, col : col + 4 * local] = grad_down[n * local : (n + 1) * local, wide_cols]
 
+    def join_quarters():
+        finish(quarter_moves)
+        placed = [quarter_recv[home] for home in homes]
+        chunks = []
+        for n in range(coarse_tiles):
+            for j in range(16):
+                lanes = slice((j % 8) * 128, (j % 8) * 128 + 128)
+                q = n * 4 + (j // 8) * 2
+                chunks.append(jnp.concatenate([placed[q][:, lanes], placed[q + 1][:, lanes]], 1))
+        moved = dot_nt(jnp.concatenate(chunks, axis=0), half_sel[...]).astype(BF16)
+        for n in range(coarse_tiles):
+            for j in range(16):
+                first = (n * 16 + j) * local
+                coarse_out[n, :, 256 * j : 256 * j + 256] = moved[first : first + local]
+
     pack_recv[pl.ds(me_c, 1)] = pack[chan_rows(me_c)][None]
     finish(to_chans(7, lambda c: pack.at[chan_rows(c)], pack_recv.at[me_c]))
     total = pack_recv[0]
@@ -528,7 +549,9 @@
         for n in range(n_pieces):
             pieces[n] = total[:, n * 128 : n * 128 + 128]
         pieces_recv[pl.ds(me_t, 1)] = pieces[pl.ds(me_t, 1)]
-        finish(to_tiles(3, lambda d: pieces.at[d], pieces_recv.at[me_t]))
+        piece_copies = to_tiles(3, lambda d: pieces.at[d], pieces_recv.at[me_t])
+        join_quarters()
+        finish(piece_copies)
         total = pieces_recv[0]
         for s in range(1, n_tile):
             total = total + pieces_recv[s]
@@ -536,31 +559,19 @@
         finish(to_tiles(4, lambda d: grads_out.at[me_t], grads_out.at[me_t]))
     else:
         pieces[pl.ds(me_t, 1)] = total[None]
-        finish(to_tiles(3, lambda d: pieces.at[me_t], pieces.at[me_t]))
+        piece_copies = to_tiles(3, lambda d: pieces.at[me_t], pieces.at[me_t])
+        join_quarters()
+        finish(piece_copies)
         total = pieces[0]
         for s in range(1, n_tile):
             total = total + pieces[s]
         for n in range(n_pieces):
             grads_out[n] = total[:, n * 128 : n * 128 + 128]
 
-    finish(quarter_copies)
-    for m in range(tiles):
-        placed_out[m] = quarter_recv[homes[m]]
-
-
-def finish_kernel(placed, grads, join_sel, coarse, grad_conv, grad_bias, grad_down):
+
+def finish_kernel(joined, grads, coarse, grad_conv, grad_bias, grad_down):
     local = coarse.shape[1]
-    chunks = []
-    for n in range(coarse.shape[0]):
-        for j in range(16):
-            lanes = slice((j % 8) * 128, (j % 8) * 128 + 128)
-            q = n * 4 + (j // 8) * 2
-            chunks.append(jnp.concatenate([placed[q, :, lanes], placed[q + 1, :, lanes]], axis=1))
-    moved = dot(jnp.concatenate(chunks, axis=0), join_sel[...]).astype(BF16)
-    for n in range(coarse.shape[0]):
-        for j in range(16):
-            first = (n * 16 + j) * local
-            coarse[n, :, 256 * j : 256 * j + 256] = moved[first : first + local]
+    coarse[...] = joined[...]
     whole = jnp.concatenate([grads[n] for n in range(grads.shape[0])], axis=1)
     grad_conv[...] = whole[:, : TAPS * C]
     grad_bias[...] = whole[:1, BIAS_COL : BIAS_COL + local]
@@ -607,10 +618,10 @@
     split = n_tile == n_pieces
     piece_shape = (n_tile, local, 128 if split else PACK)
     dma = pltpu.SemaphoreType.DMA
-    placed, grads = pl.pallas_call(
+    joined, grads = pl.pallas_call(
         functools.partial(level_kernel, n_tile, n_chan, tiles),
         out_shape=[
-            jax.ShapeDtypeStruct((tiles, local, QUARTER), BF16),
+            jax.ShapeDtypeStruct(cotangent.shape, BF16),
             jax.ShapeDtypeStruct((n_pieces, local, 128), F32),
         ],
         in_specs=[hbm] * 11 + [smem] * 6,
@@ -669,11 +680,11 @@
             jax.ShapeDtypeStruct((1, local), F32),
             jax.ShapeDtypeStruct(down_weight.shape, F32),
         ],
-        in_specs=[vmem] * 3,
+        in_specs=[vmem] * 2,
         out_specs=[vmem] * 4,
         compiler_params=pltpu.CompilerParams(vmem_limit_bytes=VMEM_LIMIT),
         name="finish",
-    )(placed, grads, const(half.T))
+    )(joined, grads)
     return (coarse, grad_conv, grad_bias.reshape(local), grad_down)
 
 

time: 52 us -> 53.2 us (1.023)
  Pallas kernels: 51.2 us -> 52.4 us
    pallas_call x1, Pallas kernels: 49.2 us -> 50.8 us  [on_device(): pl.pallas_call(functools.partial(level_kernel, n_tile, n_chan, tiles), ou...]
where the time goes in v3:
time: 53.2 us; the launch traced here: 53.1 us
  Pallas kernels  52.4 us (98%)
  between operations  0.64 us (1%)
    pallas_call x1, Pallas kernels, on_device(): pl.pallas_call(functools.partial(level_kernel, n_tile, n_chan, tiles), ou...  50.8 us
    pallas_call x1, Pallas kernels, on_device(): pl.pallas_call(finish_kernel, out_shape=[jax.ShapeDtypeStruct(cotangent.s...  1.68 us

profile of v3, /device:TPU:0, one launch (start us, length us, event | category | flops | bytes accessed | tf_op | source)
XLA Modules:
  0.0 53.1 jit_solution(14659548223485489022)
XLA Ops:
  0.6 50.8 %unet_level.1 = (bf16[2,16,4096]{2,1,0:T(8,128)(2,1)}, f32[8,16,128]{2,1,0:T(8,128)}) custom-call(bf16[8,16,4096]{2,1,0:T(8,128)(2,1)} %feat_hbm.1, bf16[2,16,4096]{2,1,0:T(8,128)(2,1)} %cot_hbm.1, bf16[16,576]{1,0:T(8,128)(2,1)} %cw_hbm.1, bf16[64,64]{1,0:T(8,128)(2,1)} %dw_hbm.1, bf16[4096,256]{1,0:T(8,128)(2,1)} %constant.14.clone.rim_sel_hbm, ...), custom_call_target="tpu_custom_call" | custom-call | tf_op jit(solution)/shard_map/unet_level/pallas_call | solution.py:621
  51.4 1.7 %finish.1 = (bf16[2,16,4096]{2,1,0:T(8,128)(2,1)}, f32[16,576]{1,0:T(8,128)}, f32[1,16]{1,0:T(1,128)}, f32[64,64]{1,0:T(8,128)}) custom-call(bf16[2,16,4096]{2,1,0:T(8,128)(2,1)} %get-tuple-element.10.joined, f32[8,16,128]{2,1,0:T(8,128)} %get-tuple-element.11.grads), custom_call_target="tpu_custom_call" | custom-call | tf_op jit(solution)/shard_map/finish/pallas_call | solution.py:675

commit v4 on v3

--- a/solution.py
+++ b/solution.py
@@ -18,6 +18,7 @@
 BF16 = jnp.bfloat16
 VMEM_LIMIT = 63 * 1024 * 1024
 PACK = 1024
+PACK_USED = 896
 FEAT = 8
 BIAS_COL = TAPS * C
 DOWN_COL = BIAS_COL + C
@@ -245,6 +246,7 @@
     quarter_send,
     quarter_recv,
     pack,
+    pack_send,
     pack_recv,
     pieces,
     pieces_recv,
@@ -487,6 +489,7 @@
         quarter_recv[pl.ds(me_t, 1)] = quarter_send[pl.ds(me_t, 1)]
         return to_tiles(2, lambda d: quarter_send.at[d], quarter_recv.at[me_t])
 
+    quarter_moves = forward_quarters()
     finish(cot_chan_copies)
     grad_wide = jnp.zeros((4 * C, 16 * C), F32)
     grad_down = jnp.zeros((C, 4 * C), F32)
@@ -498,8 +501,6 @@
         grad_down = grad_down + dot_nt(back, hidden[t])
         grad_bias = grad_bias + dot_nt(ones, grad_pre)
         grad_wide = grad_wide + dot_nt(grad_pre, window[t])
-        if t == 0:
-            quarter_moves = forward_quarters()
     taps = []
     for dy in range(3):
         for dx in range(3):
@@ -510,7 +511,8 @@
                     col = ((a + dy) * 4 + b + dx) * C
                     total = total + grad_wide[row : row + C, col : col + C]
             taps.append(total)
-    pack[:, : TAPS * C] = split_dot_nt(jnp.concatenate(taps, axis=1), tap_sel[...])
+    moved = split_dot_nt(jnp.concatenate(taps, axis=1), tap_sel[...])
+    pack[:, : TAPS * C] = moved
     pack[:, TAPS * C :] = jnp.zeros((C, PACK - TAPS * C), F32)
     grad_down = split_dot_nt(grad_down, down_sel[...].reshape(4 * C, 4 * C))
     total = grad_bias[:1, :C]
@@ -539,11 +541,13 @@
                 first = (n * 16 + j) * local
                 coarse_out[n, :, 256 * j : 256 * j + 256] = moved[first : first + local]
 
-    pack_recv[pl.ds(me_c, 1)] = pack[chan_rows(me_c)][None]
-    finish(to_chans(7, lambda c: pack.at[chan_rows(c)], pack_recv.at[me_c]))
-    total = pack_recv[0]
+    pack_send[...] = pack[:, :PACK_USED].astype(BF16)
+    pack_recv[pl.ds(me_c, 1)] = pack_send[chan_rows(me_c)][None]
+    finish(to_chans(7, lambda c: pack_send.at[chan_rows(c)], pack_recv.at[me_c]))
+    total = pack_recv[0].astype(F32)
     for c in range(1, n_chan):
-        total = total + pack_recv[c]
+        total = total + pack_recv[c].astype(F32)
+    total = jnp.concatenate([total, jnp.zeros((local, PACK - PACK_USED), F32)], axis=1)
     n_pieces = PACK // 128
     if n_tile == n_pieces:
         for n in range(n_pieces):
@@ -656,7 +660,8 @@
             pltpu.VMEM((n_tile, local, QUARTER), BF16),
             pltpu.VMEM((n_tile, local, QUARTER), BF16),
             pltpu.VMEM((C, PACK), F32),
-            pltpu.VMEM((n_chan, local, PACK), F32),
+            pltpu.VMEM((C, PACK_USED), BF16),
+            pltpu.VMEM((n_chan, local, PACK_USED), BF16),
             pltpu.VMEM(piece_shape, F32),
             pltpu.VMEM((n_tile, local, 128), F32),
             dma((13,)),

time: 53.2 us -> 52.3 us (0.983)
  Pallas kernels: 52.4 us -> 51.5 us
    pallas_call x1, Pallas kernels: 50.8 us -> 49.8 us  [on_device(): pl.pallas_call(functools.partial(level_kernel, n_tile, n_chan, tiles), ou...]
where the time goes in v4:
time: 52.3 us; the launch traced here: 52.1 us
  Pallas kernels  51.5 us (98%)
  between operations  0.64 us (1%)
    pallas_call x1, Pallas kernels, on_device(): pl.pallas_call(functools.partial(level_kernel, n_tile, n_chan, tiles), ou...  49.8 us
    pallas_call x1, Pallas kernels, on_device(): pl.pallas_call(finish_kernel, out_shape=[jax.ShapeDtypeStruct(cotangent.s...  1.68 us

profile of v4, /device:TPU:0, one launch (start us, length us, event | category | flops | bytes accessed | tf_op | source)
XLA Modules:
  0.0 52.1 jit_solution(7047303457341346367)
XLA Ops:
  0.6 49.8 %unet_level.1 = (bf16[2,16,4096]{2,1,0:T(8,128)(2,1)}, f32[8,16,128]{2,1,0:T(8,128)}) custom-call(bf16[8,16,4096]{2,1,0:T(8,128)(2,1)} %feat_hbm.1, bf16[2,16,4096]{2,1,0:T(8,128)(2,1)} %cot_hbm.1, bf16[16,576]{1,0:T(8,128)(2,1)} %cw_hbm.1, bf16[64,64]{1,0:T(8,128)(2,1)} %dw_hbm.1, bf16[4096,256]{1,0:T(8,128)(2,1)} %constant.14.clone.rim_sel_hbm, ...), custom_call_target="tpu_custom_call" | custom-call | tf_op jit(solution)/shard_map/unet_level/pallas_call | solution.py:625
  50.4 1.7 %finish.1 = (bf16[2,16,4096]{2,1,0:T(8,128)(2,1)}, f32[16,576]{1,0:T(8,128)}, f32[1,16]{1,0:T(1,128)}, f32[64,64]{1,0:T(8,128)}) custom-call(bf16[2,16,4096]{2,1,0:T(8,128)(2,1)} %get-tuple-element.10.joined, f32[8,16,128]{2,1,0:T(8,128)} %get-tuple-element.11.grads), custom_call_target="tpu_custom_call" | custom-call | tf_op jit(solution)/shard_map/finish/pallas_call | solution.py:680
